TPU v7x, 1024 devices: a whole 4x8x16 slice. The times are simulated.
1024 devices in a mesh: row: 32 (over z, y_hi), col: 32 (over y_lo, x, core).
Axes of the slice: x: 4, y: 8 (y_hi: 2, y_lo: 4; y = y_hi * 4 + y_lo), z: 16, core: 2. Of those that a mesh axis runs over, the one named last changes fastest.
Arguments:
- pmi: bfloat16 [32768, 32768], P('col', 'row'), may hold values from -0.03125 to 0.03125
- tile_mask: int32 [256, 256], P('col', 'row'), may hold values 0 or 1
- probe: bfloat16 [32768, 256], P('row', 'col'), may hold values from -6 to 6
Outputs:
- basis: float32 [32768, 256], P(('row', 'col'))
- factor: float32 [256, 256], replicated
All inputs are finite; a program needn't handle non-finite values. No bound on the sum of `tile_mask` on one device may be relied on, other than what follows from the above.
Results may differ from a plain program's by a relative error of at most 0.0021.
Values may be sent and summed in bfloat16 or wider, within the bound.
No kernel may reach another device: no remote copies, remote signals or barrier semaphores. Data moves between devices by JAX's collectives and lax.ppermute only.
A program may use at most 32 MiB of HBM per device.

v0:
```python
import math

import jax
import jax.numpy as jnp
from jax import lax
from jax.sharding import PartitionSpec as P

TILE = 128


def local(pmi, tile_mask, probe):
    rows, cols = pmi.shape
    scaled = tile_mask.astype(jnp.bfloat16)[:, None, :, None]
    masked = (pmi.reshape(rows // TILE, TILE, cols // TILE, TILE) * scaled).reshape(rows, cols)
    probe_full = lax.all_gather(probe, "col", axis=1, tiled=True)
    partial_value = jnp.dot(masked, probe_full, preferred_element_type=jnp.float32)
    sketch = lax.psum(partial_value, "row").astype(jnp.bfloat16)
    mine = lax.psum_scatter(
        lax.dot_general(
            masked, sketch, (((0,), (0,)), ((), ())), preferred_element_type=jnp.float32
        ),
        "col",
        scatter_dimension=0,
        tiled=True,
    )
    gram_part = jnp.dot(
        mine.T, mine, precision=lax.Precision.HIGHEST, preferred_element_type=jnp.float32
    )
    gram = lax.psum(gram_part, ("row", "col"))
    lower = jnp.linalg.cholesky(gram)
    solved = lax.linalg.triangular_solve(lower, mine, left_side=False, lower=True, transpose_a=True)
    basis = solved * jnp.float32(math.sqrt(cols * lax.axis_size("row")))
    return (basis, lower.T)


def solution(mesh):
    in_specs = (P("col", "row"), P("col", "row"), P("row", "col"))
    out_specs = (P(("row", "col"), None), P())
    return jax.shard_map(local, mesh=mesh, in_specs=in_specs, out_specs=out_specs, check_vma=False)
```

profile of v0, /device:TPU:1, one launch (start us, length us, event | category | flops | bytes accessed | tf_op | source)
XLA Modules:
  0.0 969.1 jit_solution(4917501588646247145)
XLA Ops:
  7.2 0.0 reduce-scatter.2.cloned.1.call-start
  7.2 0.0 copy-start.1
  7.2 0.8 convert_element_type.6
  8.1 53.3 %all_gather.3 = bf16[1024,256]{0,1:T(8,128)(2,1)S(1)} all-gather(bf16[1024,8]{0,1:T(8,128)(2,1)} %param.5), channel_id=1, replica_groups=mesh['row'=32,'col'=32] {'col'}, dimensions={1}, use_global_device_ids=true | all-gather | bytes 540672 | tf_op jit(solution)/shard_map/all_gather | solution.py:15
  61.3 0.3 mul.17
  61.7 0.0 copy-done.1
  61.7 0.7 fusion.1
  62.4 186.2 %all-reduce.5 = bf16[1024,256]{1,0:T(8,128)(2,1)} all-reduce(f32[1024,256]{1,0:T(8,128)S(1)} %fusion.1), channel_id=1, replica_groups=mesh['row'=32,'col'=32] {'row'}, use_global_device_ids=true, to_apply=%region_0.0 | all-reduce | flops 262144 | bytes 1572864 | tf_op jit(solution)/shard_map/psum | solution.py:17
  248.6 3.6 fusion
  252.2 0.0 reduce-scatter.2.cloned.1.call-update
  252.3 0.2 all-reduce.4.cloned.1.call-start
  252.5 162.9 %reduce-scatter.2.cloned.1.call-done = f32[32,256]{1,0:T(8,128)} async-done(((f32[1024,256]{1,0:T(8,128)}), f32[32,256]{1,0:T(8,128)}) %reduce-scatter.2.cloned.1.call-update) | async-done | bytes 32784 | tf_op jit(solution)/shard_map/reduce_scatter | solution.py:18
  415.4 2.0 fusion.14
  417.4 0.0 all-reduce.4.cloned.1.call-update
  417.4 0.0 copy-start
  417.4 480.8 %all-reduce.4.cloned.1.call-done = f32[256,256]{0,1:T(8,128)} async-done(((f32[256,256]{0,1:T(8,128)}), f32[256,256]{0,1:T(8,128)}) %all-reduce.4.cloned.1.call-update) | async-done | bytes 262160 | tf_op jit(solution)/shard_map/psum | solution.py:29
  898.2 1.1 copy.6
  899.3 1.0 fusion.3
  900.3 11.7 %cholesky.50 = f32[128,128]{1,0:T(8,128)S(1)} custom-call(f32[128,128]{1,0:T(8,128)S(1)} %cholesky.118), custom_call_target="Cholesky" | custom-call | tf_op jit(solution)/shard_map/jit(cholesky)/cholesky | solution.py:30
  912.0 9.8 %custom-call.14 = f32[1,128,128]{1,2,0:T(8,128)S(1)} custom-call(f32[1,128,128]{2,1,0:T(8,128)S(1)} %get-tuple-element.27), custom_call_target="InvertDiagBlocksLowerTriangular" | custom-call | tf_op jit(solution)/shard_map/jit(cholesky)/cholesky | solution.py:30
  921.9 0.2 constant_dynamic-update-slice_fusion.1
  922.1 0.3 convolution_subtract_fusion
  922.4 11.7 %cholesky.105 = f32[128,128]{1,0:T(8,128)S(1)} custom-call(f32[128,128]{1,0:T(8,128)S(1)} %convolution_subtract_fusion), custom_call_target="Cholesky" | custom-call | tf_op jit(solution)/shard_map/jit(cholesky)/cholesky | solution.py:30
  934.1 0.7 compare_reduce_fusion
  936.2 0.1 triangular_solve.58
  936.3 4.3 while.1
  936.5 0.6 fusion.24
  937.1 1.4 bitcast_dynamic-update-slice_fusion.2
  938.5 0.6 fusion.24
  939.1 1.4 bitcast_dynamic-update-slice_fusion.2
  940.6 19.7 %custom-call.15 = f32[2,128,128]{1,2,0:T(8,128)S(1)} custom-call(f32[2,128,128]{2,1,0:T(8,128)S(1)} %get-tuple-element.9), custom_call_target="InvertDiagBlocksLowerTriangular" | custom-call | tf_op jit(solution)/shard_map/triangular_solve | solution.py:31
  960.2 0.0 copy-done
  960.3 0.2 fusion.8
  960.4 0.2 convolution_subtract_fusion.1
  960.6 0.2 fusion.6
  960.8 0.6 maximum_multiply_fusion
  961.5 0.8 copy.7
  (9 shorter events, 0.2 us)
Async XLA Ops:
  7.2 408.3 %reduce-scatter.2.cloned.1.call-start = ((), (), s32[]{:S(2)}) async-start(), calls=%async_computation.1 | async-start | bytes 1081344 | tf_op jit(solution)/shard_map/reduce_scatter | solution.py:18
  7.2 54.5 %copy-start.1 = (bf16[1024,1024]{1,0:T(8,128)(2,1)S(1)}, bf16[1024,1024]{1,0:T(8,128)(2,1)}, u32[]{:S(2)}) copy-start(bf16[1024,1024]{1,0:T(8,128)(2,1)} %param.3) | copy-start | bytes 6291460
  252.3 645.9 %all-reduce.4.cloned.1.call-start = ((), (), s32[]{:S(2)}) async-start(), calls=%async_computation.2 | async-start | bytes 524288 | tf_op jit(solution)/shard_map/psum | solution.py:29
  417.4 542.8 %copy-start = (f32[32,256]{1,0:T(8,128)S(1)}, f32[32,256]{1,0:T(8,128)}, u32[]{:S(2)}) copy-start(f32[32,256]{1,0:T(8,128)} %reduce-scatter.2.cloned.1.call-done) | copy-start | bytes 98308
Sparse Core Ops, SparseCore 0:
  252.4 162.9 reduce-scatter.1
  422.3 475.7 all-reduce.3
where the time goes:
time: 971 us; the launch traced here: 969 us
  waiting for transfers between devices  644 us (66%)
  blocking collectives  239 us (25%)
  other arithmetic  56.2 us (6%)
  between operations  15.5 us (2%)
    psum x1, waiting for transfers between devices, local(): gram = lax.psum(gram_part, ('row', 'col'))  481 us
    psum x1, blocking collectives, local(): sketch = lax.psum(partial_value, 'row').astype(jnp.bfloat16)  186 us
    reduce_scatter x1, waiting for transfers between devices, local(): lax.psum_scatter(lax.dot_general(masked, sketch, (((0,), (0,)), ((), ()))...  163 us
    all_gather x1, blocking collectives, local(): probe_full = lax.all_gather(probe, 'col', axis=1, tiled=True)  53.3 us
    another operation x6, other arithmetic, local(): lower = jnp.linalg.cholesky(gram)  34 us
    another operation x2, other arithmetic, local(): lax.linalg.triangular_solve(lower, mine, left_side=False, lower=True, tra...  19.7 us
  transfers between devices with their start and end apart: 2, of which 2 were waited for; matrix products, arithmetic and copies ran while one was open for 0% of the time, Pallas kernels for 0%

commit v1 on v0

v1 whole, which is shorter than its diff:
```python
import functools
import math

import jax
import jax.numpy as jnp
from jax import lax
from jax.experimental import pallas as pl
from jax.experimental.pallas import tpu as pltpu
from jax.sharding import PartitionSpec as P

TILE = 128


def exchange(blocks, axis):
    return lax.all_to_all(blocks, axis, split_axis=0, concat_axis=0, tiled=True)


def spread(block, axis):
    n = lax.axis_size(axis)
    return exchange(jnp.broadcast_to(block[None], (n,) + block.shape), axis)


def scatter_sum(whole, axis):
    n = lax.axis_size(axis)
    rows, columns = whole.shape
    return jnp.sum(exchange(whole.reshape(n, rows // n, columns), axis), axis=0)

SUB = 8
LANES = 128
PANEL = 64


def eliminate(panel, first):
    height, width = panel.shape
    tiles = height // SUB
    rows = [panel[SUB * v : SUB * (v + 1)] for v in range(tiles)]
    sub = lax.broadcasted_iota(jnp.int32, (SUB, LANES), 0)

    def wide(a):
        return jnp.concatenate([a] * (width // LANES), axis=1)

    done = []
    for t in range(tiles):
        at = first + t * SUB
        pivots = jnp.zeros((SUB, LANES), jnp.float32)
        columns = {
            v: [jnp.broadcast_to(rows[v][:, at + k : at + k + 1], (SUB, LANES)) for k in range(SUB)]
            for v in range(t, tiles)
        }
        for k in range(SUB):
            pivot = jnp.broadcast_to(columns[t][k][k : k + 1], (SUB, LANES))
            inverse = 1.0 / pivot
            pivots = jnp.where(sub == k, pivot, pivots)
            row = jnp.broadcast_to(rows[t][k : k + 1], (SUB, width))
            heads = [jnp.broadcast_to(columns[t][l][k : k + 1], (SUB, LANES)) for l in range(k + 1, SUB)]
            for v in range(t, tiles):
                times = columns[v][k] * inverse
                if v == t:
                    times = jnp.where(sub > k, times, 0.0)
                rows[v] = rows[v] - wide(times) * row
                for l in range(k + 1, SUB):
                    columns[v][l] = columns[v][l] - times * heads[l - k - 1]
        done.append(rows[t] * wide(lax.rsqrt(pivots)))
    return jnp.concatenate(done, axis=0)


def cholesky_qr_kernel(scale, gram_ref, right_ref, factor_ref, basis_ref, work):
    n, size = right_ref.shape
    padding = jnp.zeros((LANES - n, size), jnp.float32)
    work[:, :size] = gram_ref[...]
    work[:, size:] = jnp.concatenate([right_ref[...], padding], axis=0).T
    for low in range(0, size, PANEL):
        high = low + PANEL
        panel = eliminate(work[low:high, :], low)
        work[low:high, :] = panel
        if high < size:
            base = high // LANES * LANES
            change = lax.dot_general(
                panel[:, base:size],
                panel,
                (((0,), (0,)), ((), ())),
                precision=lax.Precision.HIGHEST,
                preferred_element_type=jnp.float32,
            )
            work[high:, :] = work[high:, :] - change[high - base :]
    at_row = lax.broadcasted_iota(jnp.int32, (size, size), 0)
    at_column = lax.broadcasted_iota(jnp.int32, (size, size), 1)
    factor_ref[...] = jnp.where(at_row <= at_column, work[:, :size], 0.0)
    basis_ref[...] = work[:, size:].T[:n] * scale


def cholesky_qr(gram, right, scale):
    vmem = pl.BlockSpec(memory_space=pltpu.VMEM)
    size = gram.shape[0]
    return pl.pallas_call(
        functools.partial(cholesky_qr_kernel, scale),
        out_shape=(
            jax.ShapeDtypeStruct((size, size), jnp.float32),
            jax.ShapeDtypeStruct(right.shape, jnp.float32),
        ),
        in_specs=[vmem, vmem],
        out_specs=(vmem, vmem),
        scratch_shapes=[pltpu.VMEM((size, size + LANES), jnp.float32)],
        name="cholesky_qr",
    )(gram, right)


def local(pmi, tile_mask, probe):
    rows, cols = pmi.shape
    scaled = tile_mask.astype(jnp.bfloat16)[:, None, :, None]
    masked = (pmi.reshape(rows // TILE, TILE, cols // TILE, TILE) * scaled).reshape(rows, cols)
    probe_full = spread(probe.T, "col").reshape(-1, cols)
    k = probe_full.shape[0]
    partial_value = lax.dot_general(
        masked, probe_full, (((1,), (1,)), ((), ())), preferred_element_type=jnp.float32
    )
    sketch_rows = scatter_sum(partial_value, "row").astype(jnp.bfloat16)
    sketch = spread(sketch_rows, "row").reshape(rows, k)
    image = lax.dot_general(
        masked, sketch, (((0,), (0,)), ((), ())), preferred_element_type=jnp.float32
    )
    mine = scatter_sum(image, "col")
    gram_part = jnp.dot(
        mine.T, mine, precision=lax.Precision.HIGHEST, preferred_element_type=jnp.float32
    )
    gram_rows = jnp.sum(spread(scatter_sum(gram_part, "col"), "row"), axis=0)
    gram = spread(gram_rows, "col").reshape(k, k)
    scale = math.sqrt(cols * lax.axis_size("row"))
    factor, basis = cholesky_qr(gram, mine, scale)
    return (basis, factor)


def solution(mesh):
    in_specs = (P("col", "row"), P("col", "row"), P("row", "col"))
    out_specs = (P(("row", "col"), None), P())
    return jax.shard_map(local, mesh=mesh, in_specs=in_specs, out_specs=out_specs, check_vma=False)
```

time: 971 us -> 252 us (0.26)
  waiting for transfers between devices: 644 us -> 7.34 us
  other arithmetic: 56.2 us -> 1.18 us
  blocking collectives: 239 us -> 201 us
  starting transfers between devices: 0.26 us -> 17.7 us
  between operations: 15.5 us -> 0.72 us
  Pallas kernels: 0 us -> 10 us
    psum x1 -> x0, waiting for transfers between devices: 481 us -> none  [local(): gram = lax.psum(gram_part, ('row', 'col'))]
    all_to_all x0 -> x6, blocking collectives: none -> 201 us  [exchange(): return lax.all_to_all(blocks, axis, split_axis=0, concat_axis=0, tiled=True)]
    psum x1 -> x0, blocking collectives: 186 us -> none  [local(): sketch = lax.psum(partial_value, 'row').astype(jnp.bfloat16)]
    reduce_scatter x1 -> x0, waiting for transfers between devices: 163 us -> none  [local(): lax.psum_scatter(lax.dot_general(masked, sketch, (((0,), (0,)), ((), ()))...]
    another operation x8 -> x0, other arithmetic: 53.7 us -> none  [the longest x6 34 us: local(): lower = jnp.linalg.cholesky(gram)]
    all_gather x1 -> x0, blocking collectives: 53.3 us -> none  [local(): probe_full = lax.all_gather(probe, 'col', axis=1, tiled=True)]
    all_to_all x0 -> x1, starting transfers between devices: none -> 17.7 us  [exchange(): return lax.all_to_all(blocks, axis, split_axis=0, concat_axis=0, tiled=True)]
    pallas_call x0 -> x1, Pallas kernels: none -> 10 us  [cholesky_qr(): pl.pallas_call(functools.partial(cholesky_qr_kernel, scale), out_shape=(j...]
  transfers between devices with their start and end apart: 2 -> 1, of which waited for: 2 -> 1; matrix products, arithmetic and copies ran while one was open for 0% -> 3% of each run, Pallas kernels for 0% -> 0%
where the time goes in v1:
time: 252 us; the launch traced here: 251 us
  blocking collectives  201 us (80%)
  starting transfers between devices  17.7 us (7%)
  Pallas kernels  10 us (4%)
  local copies, waits for them, and re-layouts  9.96 us (4%)
  waiting for transfers between devices  7.34 us (3%)
  matrix products  3.39 us (1%)
    all_to_all x6, blocking collectives, exchange(): return lax.all_to_all(blocks, axis, split_axis=0, concat_axis=0, tiled=True)  201 us
    all_to_all x1, starting transfers between devices, exchange(): return lax.all_to_all(blocks, axis, split_axis=0, concat_axis=0, tiled=True)  17.7 us
    pallas_call x1, Pallas kernels, cholesky_qr(): pl.pallas_call(functools.partial(cholesky_qr_kernel, scale), out_shape=(j...  10 us
    all_to_all x1, waiting for transfers between devices, exchange(): return lax.all_to_all(blocks, axis, split_axis=0, concat_axis=0, tiled=True)  7.34 us
    unnamed x5, local copies, waits for them, and re-layouts  5.2 us
  transfers between devices with their start and end apart: 1, of which 1 were waited for; matrix products, arithmetic and copies ran while one was open for 3% of the time, Pallas kernels for 0%

profile of v1, /device:TPU:1, one launch (start us, length us, event | category | flops | bytes accessed | tf_op | source)
XLA Modules:
  0.0 251.3 jit_solution(12981500532901945809)
XLA Ops:
  0.6 1.6 broadcast_in_dim.8
  2.2 17.7 %all-to-all-start = ((bf16[32,8,1024]{2,1,0:T(8,128)(2,1)}), bf16[32,8,1024]{2,1,0:T(8,128)(2,1)S(1)}, u32[]{:S(2)}, u32[]{:S(2)}) async-start(bf16[32,8,1024]{2,1,0:T(8,128)(2,1)} %broadcast_in_dim.8), calls=%async_computation | async-start | bytes 1048576 | tf_op jit(solution)/shard_map/all_to_all | solution.py:15
  19.9 0.7 convert_element_type.10
  20.6 0.1 copy.15
  20.7 4.0 %copy.16 = bf16[1024,1024]{0,1:T(8,128)(2,1)} copy(bf16[1024,1024]{1,0:T(8,128)(2,1)} %param.3) | data formatting | bytes 4194304 | tf_op args[0]
  24.6 0.0 copy-start
  24.6 0.3 mul.11
  25.0 1.2 copy-done
  26.2 0.3 bitcast_multiply_fusion
  26.5 2.6 %copy.17 = bf16[1024,1024]{1,0:T(8,128)(2,1)} copy(bf16[1024,1024]{0,1:T(8,128)(2,1)S(1)} %bitcast_multiply_fusion) | data formatting | bytes 4194304 | tf_op jit(solution)/shard_map/mul | solution.py:111
  29.1 7.3 %all-to-all-done = bf16[32,8,1024]{2,1,0:T(8,128)(2,1)S(1)} async-done(((bf16[32,8,1024]{2,1,0:T(8,128)(2,1)}), bf16[32,8,1024]{2,1,0:T(8,128)(2,1)S(1)}, u32[]{:S(2)}, u32[]{:S(2)}) %all-to-all-start) | async-done | bytes 524320 | tf_op jit(solution)/shard_map/all_to_all | solution.py:15
  36.4 2.3 fusion
  38.8 67.9 %all_to_all.35 = f32[32,32,256]{2,1,0:T(8,128)S(1)} all-to-all(f32[32,32,256]{2,1,0:T(8,128)S(1)} %fusion), channel_id=1, replica_groups=mesh['row'=32,'col'=32] {'row'}, dimensions={0} | all-to-all | bytes 2097152 | tf_op jit(solution)/shard_map/all_to_all | solution.py:15
  106.7 0.1 reduce_sum.36
  106.7 0.1 broadcast_in_dim.9
  106.8 38.2 %all_to_all.36 = bf16[32,32,256]{2,1,0:T(8,128)(2,1)S(1)} all-to-all(bf16[32,32,256]{2,1,0:T(8,128)(2,1)S(1)} %broadcast_in_dim.9), channel_id=1, replica_groups=mesh['row'=32,'col'=32] {'row'}, dimensions={0} | all-to-all | bytes 1048576 | tf_op jit(solution)/shard_map/all_to_all | solution.py:15
  145.0 0.7 fusion.5
  145.7 33.2 %all_to_all.37 = f32[32,32,256]{2,1,0:T(8,128)S(1)} all-to-all(f32[32,32,256]{2,1,0:T(8,128)S(1)} %fusion.5), channel_id=1, replica_groups=mesh['row'=32,'col'=32] {'col'}, dimensions={0} | all-to-all | bytes 2097152 | tf_op jit(solution)/shard_map/all_to_all | solution.py:15
  178.9 0.1 reduce_sum.37.right_ref
  178.9 0.0 copy-start.1
  178.9 0.1 copy.18
  179.0 0.3 fusion.2
  179.4 16.1 %all_to_all.38 = f32[32,8,256]{2,1,0:T(8,128)S(1)} all-to-all(f32[32,8,256]{2,1,0:T(8,128)S(1)} %fusion.2), channel_id=1, replica_groups=mesh['row'=32,'col'=32] {'col'}, dimensions={0} | all-to-all | bytes 524288 | tf_op jit(solution)/shard_map/all_to_all | solution.py:15
  195.6 28.3 %all_to_all.39 = f32[32,8,256]{2,1,0:T(8,128)S(1)} all-to-all(f32[32,8,256]{2,1,0:T(8,128)S(1)} %broadcast_in_dim.10), channel_id=1, replica_groups=mesh['row'=32,'col'=32] {'row'}, dimensions={0} | all-to-all | bytes 524288 | tf_op jit(solution)/shard_map/all_to_all | solution.py:15
  224.0 17.3 %all_to_all.40 = f32[32,8,256]{2,1,0:T(8,128)} all-to-all(f32[32,8,256]{2,1,0:T(8,128)S(1)} %broadcast_in_dim.11), channel_id=1, replica_groups=mesh['row'=32,'col'=32] {'col'}, dimensions={0} | all-to-all | bytes 524288 | tf_op jit(solution)/shard_map/all_to_all | solution.py:15
  241.3 0.0 copy-done.1
  241.3 10.0 %cholesky_qr.1 = (f32[256,256]{1,0:T(8,128)}, f32[32,256]{1,0:T(8,128)}) custom-call(f32[256,256]{1,0:T(8,128)} %bitcast.34, f32[32,256]{1,0:T(8,128)} %copy-done.1), custom_call_target="tpu_custom_call" | custom-call | tf_op jit(solution)/shard_map/cholesky_qr/pallas_call | solution.py:95
  (4 shorter events, 0.1 us)
Async XLA Ops:
  2.2 34.2 %all-to-all-start = ((bf16[32,8,1024]{2,1,0:T(8,128)(2,1)}), bf16[32,8,1024]{2,1,0:T(8,128)(2,1)S(1)}, u32[]{:S(2)}, u32[]{:S(2)}) async-start(bf16[32,8,1024]{2,1,0:T(8,128)(2,1)} %broadcast_in_dim.8), calls=%async_computation | async-start | bytes 1048576 | tf_op jit(solution)/shard_map/all_to_all | solution.py:15
  24.6 1.6 copy-start
  178.9 62.3 %copy-start.1 = (f32[32,256]{1,0:T(8,128)}, f32[32,256]{1,0:T(8,128)S(1)}, u32[]{:S(2)}) copy-start(f32[32,256]{1,0:T(8,128)S(1)} %reduce_sum.37.right_ref) | copy-start | bytes 98308
